TPU v7x, 32 devices: a whole 2x2x4 slice. The times are simulated.
32 devices in a mesh: seq: 16 (over z, y, core), batch: 2 (over x).
Axes of the slice: x: 2, y: 2, z: 4, core: 2. Of those that a mesh axis runs over, the one named last changes fastest.
Arguments:
- inputs: bfloat16 [2, 8192, 1024], P('batch', 'seq'), may hold values from -6 to 6
- lengths: int32 [2], P('batch'), may hold values from 7937 to 8192, as said below
- norm_one_gain: bfloat16 [1024], replicated, may hold values from 0.099609375 to 1.8984375
- w_in: bfloat16 [1024, 3072], P(('seq', 'batch')), may hold values from -0.1875 to 0.1875
- conv_weight: bfloat16 [3, 1024], replicated, may hold values from -3 to 3
- w_out: bfloat16 [1024, 1024], P(('seq', 'batch')), may hold values from -0.1875 to 0.1875
- norm_two_gain: bfloat16 [1024], replicated, may hold values from 0.099609375 to 1.8984375
- w_gate: bfloat16 [1024, 4608], P('seq', 'batch'), may hold values from -0.1875 to 0.1875
- w_up: bfloat16 [1024, 4608], P('seq', 'batch'), may hold values from -0.1875 to 0.1875
- w_down: bfloat16 [4608, 1024], P('batch', 'seq'), may hold values from -0.1875 to 0.1875
- cotangent: bfloat16 [2, 8192, 1024], P('batch', 'seq'), may hold values from -6 to 6
Outputs:
- result: bfloat16 [2, 8192, 1024], P('batch', 'seq')
- grad_inputs: float32 [2, 8192, 1024], P('batch', 'seq')
- grad_norm_one: float32 [1024], replicated
- grad_w_in: float32 [1024, 3072], P(('seq', 'batch'))
- grad_conv: float32 [3, 1024], replicated
- grad_w_out: float32 [1024, 1024], P(('seq', 'batch'))
- grad_norm_two: float32 [1024], replicated
- grad_w_gate: float32 [1024, 4608], P('seq', 'batch')
- grad_w_up: float32 [1024, 4608], P('seq', 'batch')
- grad_w_down: float32 [4608, 1024], P('batch', 'seq')
Inputs may be any that keep to these rules, and one draw needn't show every extreme that they name: `lengths`: one sequence has length exactly 8192; every length is above 7936.
All inputs are finite; a program needn't handle non-finite values.
Results may differ from a plain program's by a relative error of at most 0.024.
Values may be sent and summed in bfloat16 or wider, within the bound.
A program may use at most 256 MiB of HBM per device.

v0:
```python
import jax
import jax.numpy as jnp
from jax import lax
from jax.sharding import PartitionSpec as P

epsilon = 1e-05


def shifted(block, axis, distance):
    devices = range(lax.axis_size(axis))
    route = [(i - distance, i) for i in devices if i - distance in devices]
    return lax.ppermute(block, axis, route)


def over_rows(left, right):
    return lax.dot_general(
        left, right, (((0,), (0,)), ((), ())), preferred_element_type=jnp.float32
    )


def by_rows(left, right):
    return lax.dot_general(
        left, right, (((1,), (1,)), ((), ())), preferred_element_type=jnp.float32
    )


def rounded_dot(left, right):
    return (
        jnp.dot(left, right, preferred_element_type=jnp.float32)
        .astype(jnp.bfloat16)
        .astype(jnp.float32)
    )


def on_device(
    inputs,
    lengths,
    norm_one_gain,
    w_in,
    conv_weight,
    w_out,
    norm_two_gain,
    w_gate,
    w_up,
    w_down,
    cotangent,
):
    in_all, out_all = (
        lax.all_gather(w_in, ("seq", "batch"), axis=0, tiled=True),
        lax.all_gather(w_out, ("seq", "batch"), axis=0, tiled=True),
    )
    gate_seq, up_seq, down_seq = (
        lax.all_gather(w_gate, "seq", axis=0, tiled=True),
        lax.all_gather(w_up, "seq", axis=0, tiled=True),
        lax.all_gather(w_down, "seq", axis=1, tiled=True),
    )
    tok_rows = inputs.shape[1]
    feat_width = inputs.shape[2]
    x_float = inputs[0].astype(jnp.float32)
    gain_one = norm_one_gain.astype(jnp.float32)
    gain_two = norm_two_gain.astype(jnp.float32)
    kernel = conv_weight.astype(jnp.float32)
    position = lax.axis_index("seq") * tok_rows + lax.iota(jnp.int32, tok_rows)
    valid_mask = (position < lengths[0]).astype(jnp.float32)[:, None]
    scale_one = lax.rsqrt(jnp.mean(x_float * x_float, axis=1, keepdims=True) + epsilon)
    hat_one = x_float * scale_one
    normed_one = (hat_one * gain_one).astype(jnp.bfloat16)
    projected = rounded_dot(normed_one, in_all)
    b_part = projected[:, :feat_width]
    c_part = projected[:, feat_width : 2 * feat_width]
    v_part = projected[:, 2 * feat_width :]
    product = (b_part * v_part).astype(jnp.bfloat16)
    carried = shifted(product[tok_rows - 2 :], "seq", 1)
    extended = jnp.concatenate([carried, product], axis=0).astype(jnp.float32)
    conv_out = (
        kernel[0] * extended[:tok_rows]
        + kernel[1] * extended[1 : tok_rows + 1]
        + kernel[2] * extended[2:]
    )
    gated_mix = (c_part * conv_out).astype(jnp.bfloat16)
    mixer_out = rounded_dot(gated_mix, out_all)
    middle = x_float + valid_mask * mixer_out
    scale_two = lax.rsqrt(jnp.mean(middle * middle, axis=1, keepdims=True) + epsilon)
    hat_two = middle * scale_two
    normed_two = (hat_two * gain_two).astype(jnp.bfloat16)
    grad_out = cotangent[0].astype(jnp.float32)
    grad_ffn = (valid_mask * grad_out).astype(jnp.bfloat16)
    gate_use, up_use, down_use = (
        lax.all_gather(gate_seq, "batch", axis=1, tiled=True),
        lax.all_gather(up_seq, "batch", axis=1, tiled=True),
        lax.all_gather(down_seq, "batch", axis=0, tiled=True),
    )
    rows_norm, rows_grad = (normed_two, grad_ffn)
    gate_val = rounded_dot(rows_norm, gate_use)
    up_val = rounded_dot(rows_norm, up_use)
    hidden = (jax.nn.silu(gate_val) * up_val).astype(jnp.bfloat16)
    partial_out = jnp.dot(hidden, down_use, preferred_element_type=jnp.float32)
    ffn_out = partial_out.astype(jnp.bfloat16).astype(jnp.float32)
    result = (middle + valid_mask * ffn_out).astype(jnp.bfloat16)
    grad_down = over_rows(hidden, rows_grad)
    grad_hidden = by_rows(rows_grad, down_use)
    sigmoid_gate = jax.nn.sigmoid(gate_val)
    silu_gate = gate_val * sigmoid_gate
    slope_gate = sigmoid_gate * (1.0 + gate_val * (1.0 - sigmoid_gate))
    grad_gate = (grad_hidden * up_val * slope_gate).astype(jnp.bfloat16)
    grad_up = (grad_hidden * silu_gate).astype(jnp.bfloat16)
    grad_gate_w = over_rows(rows_norm, grad_gate)
    grad_up_w = over_rows(rows_norm, grad_up)
    normed_part = by_rows(grad_gate, gate_use) + by_rows(grad_up, up_use)
    grad_gate_w, grad_up_w, grad_down = (
        lax.psum_scatter(
            grad_gate_w.astype(jnp.bfloat16), "batch", scatter_dimension=1, tiled=True
        ).astype(jnp.float32),
        lax.psum_scatter(
            grad_up_w.astype(jnp.bfloat16), "batch", scatter_dimension=1, tiled=True
        ).astype(jnp.float32),
        lax.psum_scatter(
            grad_down.astype(jnp.bfloat16), "batch", scatter_dimension=0, tiled=True
        ).astype(jnp.float32),
    )
    shard_gate, shard_up, shard_down = (
        lax.psum_scatter(grad_gate_w, "seq", scatter_dimension=0, tiled=True),
        lax.psum_scatter(grad_up_w, "seq", scatter_dimension=0, tiled=True),
        lax.psum_scatter(grad_down, "seq", scatter_dimension=1, tiled=True),
    )
    grad_gain_two = jnp.sum(normed_part * hat_two, axis=0)
    scaled_two = normed_part * gain_two
    grad_middle = grad_out + scale_two * (
        scaled_two - hat_two * jnp.mean(scaled_two * hat_two, axis=1, keepdims=True)
    )
    grad_mix = (valid_mask * grad_middle).astype(jnp.bfloat16)
    grad_out_w = over_rows(gated_mix, grad_mix)
    grad_gated = by_rows(grad_mix, out_all)
    grad_c = grad_gated * conv_out
    grad_conv_in = grad_gated * c_part
    grad_kernel = jnp.stack(
        [
            jnp.sum(grad_conv_in * extended[:tok_rows], axis=0),
            jnp.sum(grad_conv_in * extended[1 : tok_rows + 1], axis=0),
            jnp.sum(grad_conv_in * extended[2:], axis=0),
        ]
    )
    padded_grad = jnp.pad(grad_conv_in, ((2, 2), (0, 0)))
    grad_extended = (
        kernel[0] * padded_grad[2 : tok_rows + 4]
        + kernel[1] * padded_grad[1 : tok_rows + 3]
        + kernel[2] * padded_grad[: tok_rows + 2]
    )
    returned = shifted(grad_extended[:2], "seq", -1)
    grad_product = grad_extended[2:] + jnp.concatenate(
        [jnp.zeros((tok_rows - 2, feat_width), jnp.float32), returned], axis=0
    )
    grad_projected = jnp.concatenate(
        [grad_product * v_part, grad_c, grad_product * b_part], axis=1
    ).astype(jnp.bfloat16)
    grad_in_w = over_rows(normed_one, grad_projected)
    grad_normed_one = by_rows(grad_projected, in_all)
    shard_in, shard_out = (
        lax.psum_scatter(grad_in_w, ("seq", "batch"), scatter_dimension=0, tiled=True),
        lax.psum_scatter(grad_out_w, ("seq", "batch"), scatter_dimension=0, tiled=True),
    )
    grad_gain_one = jnp.sum(grad_normed_one * hat_one, axis=0)
    scaled_one = grad_normed_one * gain_one
    grad_inputs = grad_middle + scale_one * (
        scaled_one - hat_one * jnp.mean(scaled_one * hat_one, axis=1, keepdims=True)
    )
    total_one, total_two, total_kernel = lax.psum(
        (grad_gain_one, grad_gain_two, grad_kernel), ("seq", "batch")
    )
    return (
        result[None],
        grad_inputs[None],
        total_one,
        shard_in,
        total_kernel,
        shard_out,
        total_two,
        shard_gate,
        shard_up,
        shard_down,
    )


def solution(mesh):
    in_specs = (
        P("batch", "seq", None),
        P("batch"),
        P(),
        P(("seq", "batch"), None),
        P(),
        P(("seq", "batch"), None),
        P(),
        P("seq", "batch"),
        P("seq", "batch"),
        P("batch", "seq"),
        P("batch", "seq", None),
    )
    out_specs = (
        P("batch", "seq", None),
        P("batch", "seq", None),
        P(),
        P(("seq", "batch"), None),
        P(),
        P(("seq", "batch"), None),
        P(),
        P("seq", "batch"),
        P("seq", "batch"),
        P("batch", "seq"),
    )
    return jax.shard_map(
        on_device, mesh=mesh, in_specs=in_specs, out_specs=out_specs, check_vma=False
    )
```

profile of v0, /device:TPU:0, one launch (start us, length us, event | category | flops | bytes accessed | tf_op | source)
XLA Modules:
  0.0 1657.8 jit_solution(9974128300248169133)
XLA Ops:
  10.6 55.8 %all-gather.17.cloned.1.call-done = bf16[1024,2304]{1,0:T(8,128)(2,1)} async-done(((bf16[64,2304]{1,0:T(8,128)(2,1)}), bf16[1024,2304]{1,0:T(8,128)(2,1)}) %all-gather.17.cloned.1.call-update) | async-done | bytes 4718608 | tf_op jit(solution)/shard_map/all_gather | solution.py:54
  66.5 54.2 %all-gather.13.cloned.1.call-done = bf16[1024,2304]{1,0:T(8,128)(2,1)} async-done(((bf16[64,2304]{1,0:T(8,128)(2,1)}), bf16[1024,2304]{1,0:T(8,128)(2,1)}) %all-gather.13.cloned.1.call-update) | async-done | bytes 4718608 | tf_op jit(solution)/shard_map/all_gather | solution.py:53
  120.7 54.2 %all-gather.21.cloned.1.call-done = bf16[2304,1024]{0,1:T(8,128)(2,1)} async-done(((bf16[2304,64]{0,1:T(8,128)(2,1)}), bf16[2304,1024]{0,1:T(8,128)(2,1)}) %all-gather.21.cloned.1.call-update) | async-done | bytes 4718608 | tf_op jit(solution)/shard_map/all_gather | solution.py:55
  176.5 69.3 %all-gather.9.cloned.1.call-done = bf16[1024,3072]{1,0:T(8,128)(2,1)} async-done(((bf16[32,3072]{1,0:T(8,128)(2,1)}), bf16[1024,3072]{1,0:T(8,128)(2,1)}) %all-gather.9.cloned.1.call-update) | async-done | bytes 6291472 | tf_op jit(solution)/shard_map/all_gather | solution.py:49
  257.5 46.1 %all-gather.11.cloned.1.call-done = bf16[1024,1024]{1,0:T(8,128)(2,1)} async-done(((bf16[32,1024]{1,0:T(8,128)(2,1)}), bf16[1024,1024]{1,0:T(8,128)(2,1)}) %all-gather.11.cloned.1.call-update) | async-done | bytes 2097168 | tf_op jit(solution)/shard_map/all_gather | solution.py:50
  309.5 112.4 %all-gather.19.cloned.1.call-done = bf16[1024,4608]{1,0:T(8,128)(2,1)} async-done(((bf16[1024,2304]{1,0:T(8,128)(2,1)}), bf16[1024,4608]{1,0:T(8,128)(2,1)}) %all-gather.19.cloned.1.call-update) | async-done | bytes 9437200 | tf_op jit(solution)/shard_map/all_gather | solution.py:90
  421.9 9.3 convolution_convert_fusion.3
  431.2 110.2 %all-gather.15.cloned.1.call-done = bf16[1024,4608]{1,0:T(8,128)(2,1)} async-done(((bf16[1024,2304]{1,0:T(8,128)(2,1)}), bf16[1024,4608]{1,0:T(8,128)(2,1)}) %all-gather.15.cloned.1.call-update) | async-done | bytes 9437200 | tf_op jit(solution)/shard_map/all_gather | solution.py:89
  552.1 9.2 convolution_convert_fusion
  561.5 99.5 %all-gather.23.cloned.1.call-done = bf16[4608,1024]{0,1:T(8,128)(2,1)} async-done(((bf16[2304,1024]{0,1:T(8,128)(2,1)}), bf16[4608,1024]{0,1:T(8,128)(2,1)}) %all-gather.23.cloned.1.call-update) | async-done | bytes 9437200 | tf_op jit(solution)/shard_map/all_gather | solution.py:91
  661.0 13.9 multiply_convert_fusion
  684.6 9.7 convolution_convert_fusion.1
  694.7 9.3 fusion.38
  704.0 9.7 multiply_reduce_fusion
  738.6 35.3 %reduce-scatter.23.cloned.1.call-done = bf16[2304,1024]{1,0:T(8,128)(2,1)} async-done(((bf16[4608,1024]{1,0:T(8,128)(2,1)}), bf16[2304,1024]{1,0:T(8,128)(2,1)}) %reduce-scatter.23.cloned.1.call-update) | async-done | bytes 4718608 | tf_op jit(solution)/shard_map/reduce_scatter | solution.py:117
  781.4 105.2 %reduce-scatter.15.cloned.1.call-done = bf16[1024,2304]{1,0:T(8,128)(2,1)} async-done(((bf16[1024,4608]{1,0:T(8,128)(2,1)}), bf16[1024,2304]{1,0:T(8,128)(2,1)}) %reduce-scatter.15.cloned.1.call-update) | async-done | bytes 4718608 | tf_op jit(solution)/shard_map/reduce_scatter | solution.py:111
  893.5 106.0 %reduce-scatter.19.cloned.1.call-done = bf16[1024,2304]{1,0:T(8,128)(2,1)} async-done(((bf16[1024,4608]{1,0:T(8,128)(2,1)}), bf16[1024,2304]{1,0:T(8,128)(2,1)}) %reduce-scatter.19.cloned.1.call-update) | async-done | bytes 4718608 | tf_op jit(solution)/shard_map/reduce_scatter | solution.py:114
  1007.7 13.1 fusion.24
  1028.9 40.6 %all-reduce.2 = (f32[1024]{0:T(1024)}, f32[3,1024]{1,0:T(4,128)}, f32[1024]{0:T(1024)}) all-reduce(f32[1024]{0:T(1024)S(1)} %get-tuple-element.35, f32[3,1024]{1,0:T(4,128)S(1)} %pad_maximum_fusion.3, f32[1024]{0:T(1024)S(1)} %get-tuple-element.33), channel_id=1, replica_groups=mesh['seq'=16,'batch'=2] {'seq','batch'}, use_global_device_ids=true, to_apply=%region_5.6 | all-reduce | flops 5120 | bytes 40960 | tf_op jit(solution)/shard_map/psum | solution.py:167
  1072.9 71.6 %reduce-scatter.13.cloned.1.call-done = f32[32,1024]{1,0:T(8,128)} async-done(((f32[1024,1024]{1,0:T(8,128)}), f32[32,1024]{1,0:T(8,128)}) %reduce-scatter.13.cloned.1.call-update) | async-done | bytes 131088 | tf_op jit(solution)/shard_map/reduce_scatter | solution.py:160
  1144.5 159.0 %reduce-scatter.11.cloned.1.call-done = f32[32,3072]{1,0:T(8,128)} async-done(((f32[1024,3072]{1,0:T(8,128)}), f32[32,3072]{1,0:T(8,128)}) %reduce-scatter.11.cloned.1.call-update) | async-done | bytes 393232 | tf_op jit(solution)/shard_map/reduce_scatter | solution.py:159
  1303.6 115.6 %reduce-scatter.25.cloned.1.call-done = f32[64,2304]{1,0:T(8,128)} async-done(((f32[1024,2304]{1,0:T(8,128)}), f32[64,2304]{1,0:T(8,128)}) %reduce-scatter.25.cloned.1.call-update) | async-done | bytes 589840
  1419.1 115.7 %reduce-scatter.17.cloned.1.call-done = f32[64,2304]{1,0:T(8,128)} async-done(((f32[1024,2304]{1,0:T(8,128)}), f32[64,2304]{1,0:T(8,128)}) %reduce-scatter.17.cloned.1.call-update) | async-done | bytes 589840 | tf_op jit(solution)/shard_map/reduce_scatter | solution.py:122
  1534.8 116.2 %reduce-scatter.21.cloned.1.call-done = f32[64,2304]{1,0:T(8,128)} async-done(((f32[1024,2304]{1,0:T(8,128)}), f32[64,2304]{1,0:T(8,128)}) %reduce-scatter.21.cloned.1.call-update) | async-done | bytes 589840 | tf_op jit(solution)/shard_map/reduce_scatter | solution.py:123
  (121 shorter events, 101.3 us)
Async XLA Ops:
  7.2 59.2 %all-gather.17.cloned.1.call-start = ((), (), s32[]{:S(2)}) async-start(), calls=%async_computation.12 | async-start | bytes 5013504 | tf_op jit(solution)/shard_map/all_gather | solution.py:54
  7.9 112.8 %all-gather.13.cloned.1.call-start = ((), (), s32[]{:S(2)}) async-start(), calls=%async_computation.10 | async-start | bytes 5013504 | tf_op jit(solution)/shard_map/all_gather | solution.py:53
  8.7 166.3 %all-gather.21.cloned.1.call-start = ((), (), s32[]{:S(2)}) async-start(), calls=%async_computation.14 | async-start | bytes 5013504 | tf_op jit(solution)/shard_map/all_gather | solution.py:55
  9.4 236.4 %all-gather.9.cloned.1.call-start = ((), (), s32[]{:S(2)}) async-start(), calls=%async_computation.8 | async-start | bytes 6488064 | tf_op jit(solution)/shard_map/all_gather | solution.py:49
  10.0 293.6 %all-gather.11.cloned.1.call-start = ((), (), s32[]{:S(2)}) async-start(), calls=%async_computation.9 | async-start | bytes 2162688 | tf_op jit(solution)/shard_map/all_gather | solution.py:50
  10.6 411.3 %all-gather.19.cloned.1.call-start = ((), (), s32[]{:S(2)}) async-start(), calls=%async_computation.13 | async-start | bytes 14155776 | tf_op jit(solution)/shard_map/all_gather | solution.py:90
  66.4 475.0 %all-gather.15.cloned.1.call-start = ((), (), s32[]{:S(2)}) async-start(), calls=%async_computation.11 | async-start | bytes 14155776 | tf_op jit(solution)/shard_map/all_gather | solution.py:89
  120.7 540.3 %all-gather.23.cloned.1.call-start = ((), (), s32[]{:S(2)}) async-start(), calls=%async_computation.15 | async-start | bytes 14155776 | tf_op jit(solution)/shard_map/all_gather | solution.py:91
  175.0 598.9 %reduce-scatter.23.cloned.1.call-start = ((), (), s32[]{:S(2)}) async-start(), calls=%async_computation.22 | async-start | bytes 14155776 | tf_op jit(solution)/shard_map/reduce_scatter | solution.py:117
  251.8 3.0 collective-permute-start
  541.4 10.6 copy-start.22
  561.3 325.3 %reduce-scatter.15.cloned.1.call-start = ((), (), s32[]{:S(2)}) async-start(), calls=%async_computation.18 | async-start | bytes 14155776 | tf_op jit(solution)/shard_map/reduce_scatter | solution.py:111
  661.0 16.0 copy-start.15
  684.6 314.9 %reduce-scatter.19.cloned.1.call-start = ((), (), s32[]{:S(2)}) async-start(), calls=%async_computation.20 | async-start | bytes 14155776 | tf_op jit(solution)/shard_map/reduce_scatter | solution.py:114
  694.4 450.1 %reduce-scatter.13.cloned.1.call-start = ((), (), s32[]{:S(2)}) async-start(), calls=%async_computation.17 | async-start | bytes 4325376 | tf_op jit(solution)/shard_map/reduce_scatter | solution.py:160
  718.9 584.7 %reduce-scatter.11.cloned.1.call-start = ((), (), s32[]{:S(2)}) async-start(), calls=%async_computation.16 | async-start | bytes 12976128 | tf_op jit(solution)/shard_map/reduce_scatter | solution.py:159
  726.4 3.1 collective-permute-start.1
  738.5 680.6 %reduce-scatter.25.cloned.1.call-start = ((), (), s32[]{:S(2)}) async-start(), calls=%async_computation.23 | async-start | bytes 10027008
  781.3 753.5 %reduce-scatter.17.cloned.1.call-start = ((), (), s32[]{:S(2)}) async-start(), calls=%async_computation.19 | async-start | bytes 10027008 | tf_op jit(solution)/shard_map/reduce_scatter | solution.py:122
  893.2 757.8 %reduce-scatter.21.cloned.1.call-start = ((), (), s32[]{:S(2)}) async-start(), calls=%async_computation.21 | async-start | bytes 10027008 | tf_op jit(solution)/shard_map/reduce_scatter | solution.py:123
  1007.6 13.1 copy-start.10
  1007.7 13.1 copy-start.12
  1007.7 13.1 copy-start.14
  1020.8 48.6 %copy-start.2 = (f32[512,1024]{1,0:T(8,128)S(1)}, f32[512,1024]{1,0:T(8,128)}, u32[]{:S(2)}) copy-start(f32[512,1024]{1,0:T(8,128)} %copy-done.1) | copy-start | bytes 6291460
  (20 other events, 75.0 us)
Sparse Core Ops, SparseCore 0:
  10.3 56.0 all-gather.16
  68.7 51.9 all-gather.12
  123.0 51.9 all-gather.20
  177.7 68.0 all-gather.8
  248.6 54.9 all-gather.10
  305.0 116.8 all-gather.18
  423.4 117.9 all-gather.14
  543.0 117.9 all-gather.22
  663.3 110.5 reduce-scatter.22
  776.0 110.5 reduce-scatter.14
  888.9 110.5 reduce-scatter.18
  1002.2 142.2 reduce-scatter.12
  1151.1 152.3 reduce-scatter.10
  1308.7 110.4 reduce-scatter.24
  1423.7 111.0 reduce-scatter.16
  1539.9 111.0 reduce-scatter.20
where the time goes:
time: 1660 us
  waiting for transfers between devices  1430 us (86%)
  matrix products  121 us (7%)
  blocking collectives  40.6 us (2%)
  other arithmetic  26.2 us (2%)
  local copies, waits for them, and re-layouts  18.1 us (1%)
    reduce_scatter x1, waiting for transfers between devices, on_device(): lax.psum_scatter(grad_in_w, ('seq', 'batch'), scatter_dimension=0, tiled=...  159 us
    unnamed x17, waiting for transfers between devices  119 us
    reduce_scatter x1, waiting for transfers between devices, on_device(): lax.psum_scatter(grad_up_w, 'seq', scatter_dimension=0, tiled=True)  116 us
    reduce_scatter x1, waiting for transfers between devices, on_device(): lax.psum_scatter(grad_gate_w, 'seq', scatter_dimension=0, tiled=True)  116 us
    all_gather x1, waiting for transfers between devices, on_device(): lax.all_gather(up_seq, 'batch', axis=1, tiled=True)  112 us
    all_gather x1, waiting for transfers between devices, on_device(): lax.all_gather(gate_seq, 'batch', axis=1, tiled=True)  110 us
    reduce_scatter x1, waiting for transfers between devices, on_device(): lax.psum_scatter(grad_up_w.astype(jnp.bfloat16), 'batch', scatter_dimensi...  106 us
    reduce_scatter x1, waiting for transfers between devices, on_device(): lax.psum_scatter(grad_gate_w.astype(jnp.bfloat16), 'batch', scatter_dimen...  105 us
  transfers between devices with their start and end apart: 18, of which 18 were waited for; matrix products, arithmetic and copies ran while one was open for 9% of the time, Pallas kernels for 0%

commit v1 on v0

v1 whole, which is shorter than its diff:
```python
import functools

import jax
import jax.numpy as jnp
from jax import lax
from jax.experimental import pallas as pl
from jax.experimental.pallas import tpu as pltpu
from jax.sharding import PartitionSpec as P

epsilon = 1e-05
MESH = pl.DeviceIdType.MESH
F32, BF16 = jnp.float32, jnp.bfloat16
DEPTH = 4
PARTS = (512, 384, 256)


def over_rows(left, right):
    return lax.dot_general(
        left, right, (((0,), (0,)), ((), ())), preferred_element_type=F32
    )


def by_rows(left, right):
    return lax.dot_general(
        left, right, (((1,), (1,)), ((), ())), preferred_element_type=F32
    )


def dot(left, right):
    return jnp.dot(left, right, preferred_element_type=F32)


def rounded_dot(left, right):
    return dot(left, right).astype(BF16).astype(F32)


class Place:
    def __init__(self):
        self.s = lax.axis_index("seq")
        self.x = lax.axis_index("batch")
        self.z = self.s // 4
        self.y = (self.s // 2) % 2
        self.c = self.s % 2
        self.own = {"y": self.y, "c": self.c, "x": self.x}
        self.device = {
            "c": (self.s + 1 - 2 * self.c, self.x),
            "y": (self.s + 2 - 4 * self.y, self.x),
            "x": (self.s, 1 - self.x),
            "up": (self.s + 4, self.x),
            "down": (self.s - 4, self.x),
            "pair": (self.s + 4 - 8 * (self.z % 2), self.x),
            "far": (self.s + 8 - 16 * (self.z // 2), self.x),
        }

    def greet(self, names):
        barrier = pltpu.get_barrier_semaphore()
        ends = {"up": self.z < DEPTH - 1, "down": self.z > 0}

        def signal(name):
            pl.semaphore_signal(
                barrier, inc=1, device_id=self.device[name], device_id_type=MESH
            )

        expected = 0
        for name in names:
            if name in ends:
                pl.when(ends[name])(functools.partial(signal, name))
                expected = expected + ends[name].astype(jnp.int32)
            else:
                signal(name)
                expected = expected + 1
        pl.semaphore_wait(barrier, expected)


class Links:
    def __init__(self, place, send, recv):
        self.place, self.send, self.recv = place, send, recv
        self.used = 0

    def take(self, count):
        first = self.used
        self.used += count
        return first

    def copy(self, source, target, index, name):
        return pltpu.make_async_remote_copy(
            src_ref=source,
            dst_ref=target,
            send_sem=self.send.at[index],
            recv_sem=self.recv.at[index],
            device_id=self.place.device[name],
            device_id_type=MESH,
        )


class Gather:
    def __init__(self, links, view, stages):
        self.links, self.view, self.stages = links, view, stages
        self.place = links.place
        self.rows = {name: links.take(DEPTH) for name in ["up", "down"] + stages}

    def block(self, stage, level, theirs=False):
        where = dict(self.place.own)
        if stage is not None:
            for name in self.stages[:stage]:
                where[name] = slice(None)
            if theirs:
                where[self.stages[stage]] = 1 - where[self.stages[stage]]
        return self.view(level, where["y"], where["c"], where["x"])

    def line(self, name, level):
        ref = self.block(None, level)
        return self.links.copy(ref, ref, self.rows[name] + level, name)

    def staged(self, stage, level, theirs=False):
        name = self.stages[stage]
        ref = self.block(stage, level, theirs)
        return self.links.copy(ref, ref, self.rows[name] + level, name)

    def begin(self):
        z = self.place.z

        @pl.when(z < DEPTH - 1)
        def _():
            self.line("up", z).start()

        @pl.when(z > 0)
        def _():
            self.line("down", z).start()

        self.staged(0, z).start()

    def along(self, distance):
        z = self.place.z

        @pl.when(z >= distance)
        def _():
            level = z - distance
            self.line("up", level).wait_recv()

            @pl.when(z < DEPTH - 1)
            def _():
                self.line("up", level).start()

            self.staged(0, level).start()

        @pl.when(z + distance < DEPTH)
        def _():
            level = z + distance
            self.line("down", level).wait_recv()

            @pl.when(z > 0)
            def _():
                self.line("down", level).start()

            self.staged(0, level).start()

    def across(self, stage, distance):
        z = self.place.z

        def pass_on(level):
            self.staged(stage, level, True).wait_recv()
            if stage + 1 < len(self.stages):
                self.staged(stage + 1, level).start()

        if distance == 0:
            pass_on(z)
            return
        pl.when(z >= distance)(lambda: pass_on(z - distance))
        pl.when(z + distance < DEPTH)(lambda: pass_on(z + distance))

    def steps(self):
        found = []
        count = len(self.stages)
        for time in range(DEPTH + count):
            for stage in range(count, 0, -1):
                if 0 <= time - stage < DEPTH:
                    found.append(functools.partial(self.across, stage - 1, time - stage))
            if 0 < time < DEPTH:
                found.append(functools.partial(self.along, time))
        return found

    def drain(self):
        z = self.place.z
        for level in range(DEPTH):

            @pl.when((z >= level) & (z < DEPTH - 1))
            def _():
                self.line("up", level).wait_send()

            @pl.when((z <= level) & (z > 0))
            def _():
                self.line("down", level).wait_send()

            for stage in range(len(self.stages)):
                self.staged(stage, level).wait_send()


def add_into(target, source):
    target[...] = (target[...].astype(F32) + source[...].astype(F32)).astype(BF16)


class Reduce:
    def __init__(self, links, view, stages, slots, line_slots):
        self.links, self.view, self.stages = links, view, stages
        self.slots, self.line_slots = slots, line_slots
        self.place = links.place
        self.rows = {name: links.take(DEPTH) for name in ["up", "down"] + stages}

    def block(self, stage, level, theirs=False):
        where = dict(self.place.own)
        for name in self.stages[stage + 1 :]:
            where[name] = slice(None)
        if theirs:
            where[self.stages[stage]] = 1 - where[self.stages[stage]]
        return self.view(level, where["y"], where["c"], where["x"])

    def staged(self, stage, level):
        name = self.stages[stage]
        return self.links.copy(
            self.block(stage, level, True),
            self.slots[stage].at[level],
            self.rows[name] + level,
            name,
        )

    def line(self, name, level):
        slot = level if name == "down" else level + 1
        return self.links.copy(
            self.block(len(self.stages) - 1, level),
            self.line_slots.at[slot],
            self.rows[name] + level,
            name,
        )

    def levels(self, distance, action):
        z = self.place.z
        if distance == 0:
            action(z)
            return
        pl.when(z >= distance)(lambda: action(z - distance))
        pl.when(z + distance < DEPTH)(lambda: action(z + distance))

    def begin(self, distance):
        self.levels(distance, lambda level: self.staged(0, level).start())

    def across(self, stage, distance):
        def take(level):
            self.staged(stage, level).wait_recv()
            add_into(self.block(stage, level), self.slots[stage].at[level])
            if stage + 1 < len(self.stages):
                self.staged(stage + 1, level).start()

        self.levels(distance, take)

    def take(self, name, level):
        self.line(name, level).wait_recv()
        slot = level if name == "down" else level + 1
        add_into(
            self.block(len(self.stages) - 1, level), self.line_slots.at[slot]
        )

    def along(self, distance):
        z = self.place.z
        if distance == 0:
            pl.when(z < DEPTH - 1)(lambda: self.take("down", z))
            pl.when(z > 0)(lambda: self.take("up", z))
            return

        @pl.when(z >= distance)
        def _():
            level = z - distance
            pl.when(z < DEPTH - 1)(lambda: self.take("down", level))
            self.line("down", level).start()

        @pl.when(z + distance < DEPTH)
        def _():
            level = z + distance
            pl.when(z > 0)(lambda: self.take("up", level))
            self.line("up", level).start()

    def steps(self):
        found = []
        count = len(self.stages)
        for time in range(DEPTH + count):
            for stage in range(count, -1, -1):
                if 0 <= time - stage < DEPTH:
                    distance = DEPTH - 1 - (time - stage)
                    if stage == count:
                        found.append(functools.partial(self.along, distance))
                    else:
                        found.append(functools.partial(self.across, stage, distance))
        return found

    def drain(self):
        z = self.place.z
        for level in range(DEPTH):

            @pl.when(z > level)
            def _():
                self.line("down", level).wait_send()

            @pl.when(z < level)
            def _():
                self.line("up", level).wait_send()

            for stage in range(len(self.stages)):
                self.staged(stage, level).wait_send()


def gather_kernel(mixer_ref, f0_ref, f1_ref, f2_ref, wm, w0, w1, w2, send, recv):
    place = Place()
    links = Links(place, send, recv)
    half = mixer_ref.shape[1] // 2
    parts = [
        Gather(
            links,
            lambda z, y, c, x: wm.at[z, y, c, x, :, pl.ds(0, half)],
            ["y", "x", "c"],
        ),
        Gather(
            links,
            lambda z, y, c, x: wm.at[z, y, c, x, :, pl.ds(half, half)],
            ["x", "y", "c"],
        ),
    ]
    ffn = []
    for buffer in (w0, w1, w2):
        ffn.append(Gather(links, lambda z, y, c, x, b=buffer: b.at[z, y], ["y"]))
    twins = []
    for source, target in ((f0_ref, w0), (f1_ref, w1), (f2_ref, w2)):
        twins.append(
            links.copy(
                source.at[1 - place.c],
                target.at[place.z, place.y, place.c],
                links.take(1),
                "c",
            )
        )
    place.greet(["c", "y", "x", "up", "down"])
    wm[place.z, place.y, place.c, place.x] = mixer_ref[...]
    for part in parts:
        part.begin()
    for twin in twins:
        twin.start()
    for source, target in ((f0_ref, w0), (f1_ref, w1), (f2_ref, w2)):
        target[place.z, place.y, place.c] = source[place.c]
    first, second = parts[0].steps(), parts[1].steps()
    for step_one, step_two in zip(first, second):
        step_one()
        step_two()
    for twin, part in zip(twins, ffn):
        twin.wait_recv()
        part.begin()
        for step in part.steps():
            step()
    for part in parts + ffn:
        part.drain()
    for twin in twins:
        twin.wait_send()


def gather_all(mixer, ffn):
    columns = mixer.shape[1]
    shapes = [jax.ShapeDtypeStruct((DEPTH, 2, 2, 2, 32, columns), BF16)]
    for block in ffn:
        shapes.append(
            jax.ShapeDtypeStruct((DEPTH, 2, 2, 64, block.shape[2]), BF16)
        )
    vmem = pl.BlockSpec(memory_space=pltpu.VMEM)
    return pl.pallas_call(
        gather_kernel,
        out_shape=shapes,
        in_specs=[vmem] * 4,
        out_specs=[vmem] * 4,
        scratch_shapes=[
            pltpu.SemaphoreType.DMA((96,)),
            pltpu.SemaphoreType.DMA((96,)),
        ],
        compiler_params=pltpu.CompilerParams(
            collective_id=0, has_side_effects=True, vmem_limit_bytes=40 * 2**20
        ),
    )(mixer, *ffn)


def ffn_kernel(
    normed_ref,
    grad_ref,
    w0_ref,
    w1_ref,
    w2_ref,
    out_ref,
    back_ref,
    d0_ref,
    d1_ref,
    d2_ref,
    tokens,
    grads,
    tokens_t,
    grads_t,
    w0,
    w1,
    w2,
    r0,
    r1,
    r2,
    l0,
    l1,
    l2,
    hidden,
    slopes,
    out_sum,
    back_sum,
    out_slots,
    back_slots,
    e0,
    e1,
    e2,
    load_sem,
    send,
    recv,
):
    place = Place()
    links = Links(place, send, recv)
    rows = normed_ref.shape[0]
    weights = (w0, w1, w2)
    loads = [
        pltpu.make_async_copy(source, target, load_sem.at[i])
        for i, (source, target) in enumerate(
            zip((w0_ref, w1_ref, w2_ref), weights)
        )
    ]
    for load in loads:
        load.start()

    def share(buffer):
        first = links.take(3)
        return (
            links.copy(buffer.at[0], buffer.at[1], first, "c"),
            links.copy(buffer.at[0], buffer.at[2], first + 1, "x"),
            links.copy(buffer.at[2], buffer.at[3], first + 2, "c"),
        )

    def give_back(total, slots):
        first = links.take(3)
        return (
            links.copy(total.at[3], slots.at[2], first, "c"),
            links.copy(total.at[2], slots.at[1], first + 1, "x"),
            links.copy(total.at[1], slots.at[0], first + 2, "c"),
        )

    shared = [share(tokens), share(grads)]
    returned = [give_back(back_sum, back_slots), give_back(out_sum, out_slots)]
    reduces = [
        Reduce(links, lambda z, y, c, x, b=w: b.at[z, y], ["y"], [r], l)
        for w, r, l in zip(weights, (r0, r1, r2), (l0, l1, l2))
    ]
    twins = links.take(3)
    place.greet(["c", "y", "x", "up", "down"])
    tokens[0] = normed_ref[...]
    grads[0] = grad_ref[...]
    for group in shared:
        group[1].start()
        group[0].start()
    for group in shared:
        group[1].wait_recv()
        group[2].start()
    for group in shared:
        group[0].wait_recv()
        group[2].wait_recv()
    for load in loads:
        load.wait()

    def flip(i, carry):
        tokens_t[:, pl.ds(pl.multiple_of(i * rows, rows), rows)] = tokens[i].T
        grads_t[:, pl.ds(pl.multiple_of(i * rows, rows), rows)] = grads[i].T
        return carry

    lax.fori_loop(0, 4, flip, 0)
    depth = tokens_t.shape[0]
    for number, (weight, width) in enumerate(zip(weights, PARTS)):

        def block(i, carry, weight=weight, width=width, number=number):
            gate_up = weight[..., : 2 * width].reshape(depth, 2 * width)
            both = dot(tokens[i], gate_up).astype(BF16).astype(F32)
            gate, up = both[:, :width], both[:, width:]
            sigmoid = jax.nn.sigmoid(gate)
            silu = gate * sigmoid
            slope = sigmoid * (1.0 + gate * (1.0 - sigmoid))
            kept = (silu * up).astype(BF16)
            down = weight[..., 2 * width :].reshape(depth, width)
            grad_hidden = dot(grads[i], down)
            grad_gate = (grad_hidden * up * slope).astype(BF16)
            grad_up = (grad_hidden * silu).astype(BF16)
            where = pl.ds(pl.multiple_of(i * rows, rows), rows)
            hidden[where, :width] = kept
            slopes[where, :width] = grad_gate
            slopes[where, width : 2 * width] = grad_up
            out_part = by_rows(kept, down)
            back_part = by_rows(slopes[where, : 2 * width], gate_up)
            if number == 0:
                out_sum[i] = out_part.astype(BF16)
                back_sum[i] = back_part.astype(BF16)
            else:
                out_sum[i] = (out_sum[i].astype(F32) + out_part).astype(BF16)
                back_sum[i] = (back_sum[i].astype(F32) + back_part).astype(BF16)
            return carry

        lax.fori_loop(0, 4, block, 0)
        step = 256
        for start in range(0, 2 * width, step):
            part = dot(tokens_t[...], slopes[:, start : start + step])
            weight[..., start : start + step] = part.astype(BF16).reshape(
                weight.shape[:-1] + (step,)
            )
        for start in range(0, width, step):
            size = min(step, width - start)
            part = dot(grads_t[...], hidden[:, start : start + size])
            weight[..., 2 * width + start : 2 * width + start + size] = part.astype(
                BF16
            ).reshape(weight.shape[:-1] + (size,))
        for distance in (3, 2, 1, 0):
            reduces[number].begin(distance)

    for total, slots, group in zip(
        (back_sum, out_sum), (back_slots, out_slots), returned
    ):
        group[0].start()
        group[2].start()
    for total, slots, group in zip(
        (back_sum, out_sum), (back_slots, out_slots), returned
    ):
        group[0].wait_recv()
        add_into(total.at[2], slots.at[2])
        group[1].start()
    for reduce in reduces:
        for action in reduce.steps():
            action()
    for total, slots, group, target in zip(
        (back_sum, out_sum),
        (back_slots, out_slots),
        returned,
        (back_ref, out_ref),
    ):
        group[1].wait_recv()
        group[2].wait_recv()
        target[...] = (
            total[0].astype(F32) + slots[0].astype(F32) + slots[1].astype(F32)
        )
    exchanges = []
    for number, (weight, edge, target) in enumerate(
        zip(weights, (e0, e1, e2), (d0_ref, d1_ref, d2_ref))
    ):
        edge[...] = weight[place.z, place.y, 1 - place.c]
        exchange = links.copy(
            edge, target.at[place.c], twins + number, "c"
        )
        exchange.start()
        target[place.c] = weight[place.z, place.y, place.c]
        exchanges.append(exchange)
    for exchange in exchanges:
        exchange.wait()
    for reduce in reduces:
        reduce.drain()
    for group in shared + returned:
        for copy in group:
            copy.wait_send()


def ffn_all(normed, grad, weights):
    rows, depth = normed.shape
    vmem = pl.BlockSpec(memory_space=pltpu.VMEM)
    hbm = pl.BlockSpec(memory_space=pl.ANY)
    out_shape = [
        jax.ShapeDtypeStruct((rows, depth), F32),
        jax.ShapeDtypeStruct((rows, depth), F32),
    ] + [jax.ShapeDtypeStruct((2, 64, 3 * w), BF16) for w in PARTS]
    block = (128 // 64, 64)
    scratch = (
        [pltpu.VMEM((4, rows, depth), BF16)] * 2
        + [pltpu.VMEM((depth, 4 * rows), BF16)] * 2
        + [pltpu.VMEM((DEPTH, 2) + block + (3 * w,), BF16) for w in PARTS]
        + [pltpu.VMEM((DEPTH,) + block + (3 * w,), BF16) for w in PARTS]
        + [pltpu.VMEM((DEPTH + 1,) + block + (3 * w,), BF16) for w in PARTS]
        + [
            pltpu.VMEM((4 * rows, PARTS[0]), BF16),
            pltpu.VMEM((4 * rows, 2 * PARTS[0]), BF16),
        ]
        + [pltpu.VMEM((4, rows, depth), BF16)] * 2
        + [pltpu.VMEM((3, rows, depth), BF16)] * 2
        + [pltpu.VMEM((64, 3 * w), BF16) for w in PARTS]
        + [
            pltpu.SemaphoreType.DMA((3,)),
            pltpu.SemaphoreType.DMA((64,)),
            pltpu.SemaphoreType.DMA((64,)),
        ]
    )
    return pl.pallas_call(
        ffn_kernel,
        out_shape=out_shape,
        in_specs=[vmem, vmem, hbm, hbm, hbm],
        out_specs=[vmem] * 5,
        scratch_shapes=scratch,
        compiler_params=pltpu.CompilerParams(
            collective_id=1, has_side_effects=True, vmem_limit_bytes=63 * 2**20
        ),
    )(normed, grad, *weights)


def reduce_kernel(
    grad_ref, small_ref, own_ref, sum_ref, work, c0, c1, a0, a1, b0, b1, z0, z1,
    small, load_sem, send, recv,
):
    place = Place()
    links = Links(place, send, recv)
    load = pltpu.make_async_copy(grad_ref, work, load_sem)
    load.start()
    half = work.shape[-1] // 2
    parts = [
        Reduce(
            links,
            lambda z, y, c, x: work.at[z, y, c, x, :, pl.ds(0, half)],
            ["c", "x", "y"],
            [c0, a0, b0],
            z0,
        ),
        Reduce(
            links,
            lambda z, y, c, x: work.at[z, y, c, x, :, pl.ds(half, half)],
            ["c", "y", "x"],
            [c1, a1, b1],
            z1,
        ),
    ]
    ring = ("c", "x", "y", "pair", "far")
    first = links.take(len(ring))
    place.greet(["c", "y", "x", "up", "down", "far"])
    load.wait()
    for distance in (3, 2, 1, 0):
        for part in parts:
            part.begin(distance)
    small[0] = small_ref[...]
    rounds = [
        links.copy(small.at[i], small.at[len(ring) + 1 + i], first + i, name)
        for i, name in enumerate(ring)
    ]
    steps = list(zip(parts[0].steps(), parts[1].steps()))
    rounds[0].start()
    for number, (one, two) in enumerate(steps):
        one()
        two()
        if number < len(ring):
            rounds[number].wait_recv()
            small[number + 1] = small[number] + small[len(ring) + 1 + number]
            if number + 1 < len(ring):
                rounds[number + 1].start()
    sum_ref[...] = small[len(ring)]
    own_ref[...] = work[place.z, place.y, place.c, place.x].astype(F32)
    for part in parts:
        part.drain()
    for copy in rounds:
        copy.wait_send()


def reduce_all(grad, small):
    columns = grad.shape[-1]
    half = columns // 2
    vmem = pl.BlockSpec(memory_space=pltpu.VMEM)
    hbm = pl.BlockSpec(memory_space=pl.ANY)
    return pl.pallas_call(
        reduce_kernel,
        out_shape=[
            jax.ShapeDtypeStruct((32, columns), F32),
            jax.ShapeDtypeStruct(small.shape, F32),
        ],
        in_specs=[hbm, vmem],
        out_specs=[vmem, vmem],
        scratch_shapes=[pltpu.VMEM(grad.shape, BF16)]
        + [pltpu.VMEM((DEPTH, 2, 2, 32, half), BF16)] * 2
        + [pltpu.VMEM((DEPTH, 2, 32, half), BF16)] * 2
        + [pltpu.VMEM((DEPTH, 32, half), BF16)] * 2
        + [pltpu.VMEM((DEPTH + 1, 32, half), BF16)] * 2
        + [
            pltpu.VMEM((11,) + small.shape, F32),
            pltpu.SemaphoreType.DMA,
            pltpu.SemaphoreType.DMA((64,)),
            pltpu.SemaphoreType.DMA((64,)),
        ],
        compiler_params=pltpu.CompilerParams(
            collective_id=2, has_side_effects=True, vmem_limit_bytes=40 * 2**20
        ),
    )(grad, small)


def shifted(block, axis, distance):
    devices = range(lax.axis_size(axis))
    route = [(i - distance, i) for i in devices if i - distance in devices]
    return lax.ppermute(block, axis, route)


def mixer_forward(inputs, lengths, norm_one_gain, conv_weight, norm_two_gain, in_all, out_all):
    tok_rows, feat_width = inputs.shape[1:]
    kept = {}
    x_float = inputs[0].astype(F32)
    kernel = conv_weight.astype(F32)
    position = lax.axis_index("seq") * tok_rows + lax.iota(jnp.int32, tok_rows)
    valid_mask = (position < lengths[0]).astype(F32)[:, None]
    scale_one = lax.rsqrt(jnp.mean(x_float * x_float, axis=1, keepdims=True) + epsilon)
    hat_one = x_float * scale_one
    normed_one = (hat_one * norm_one_gain.astype(F32)).astype(BF16)
    projected = rounded_dot(normed_one, in_all)
    b_part = projected[:, :feat_width]
    c_part = projected[:, feat_width : 2 * feat_width]
    v_part = projected[:, 2 * feat_width :]
    product = (b_part * v_part).astype(BF16)
    carried = shifted(product[tok_rows - 2 :], "seq", 1)
    extended = jnp.concatenate([carried, product], axis=0).astype(F32)
    conv_out = (
        kernel[0] * extended[:tok_rows]
        + kernel[1] * extended[1 : tok_rows + 1]
        + kernel[2] * extended[2:]
    )
    gated_mix = (c_part * conv_out).astype(BF16)
    mixer_out = rounded_dot(gated_mix, out_all)
    middle = x_float + valid_mask * mixer_out
    scale_two = lax.rsqrt(jnp.mean(middle * middle, axis=1, keepdims=True) + epsilon)
    hat_two = middle * scale_two
    normed_two = (hat_two * norm_two_gain.astype(F32)).astype(BF16)
    kept.update(locals())
    return kept


def mixer_backward(kept, grad_out, normed_part, norm_one_gain, norm_two_gain, in_all, out_all):
    tok_rows, feat_width = grad_out.shape
    kernel = kept["kernel"]
    extended, conv_out = kept["extended"], kept["conv_out"]
    hat_one, hat_two = kept["hat_one"], kept["hat_two"]
    grad_gain_two = jnp.sum(normed_part * hat_two, axis=0)
    scaled_two = normed_part * norm_two_gain.astype(F32)
    grad_middle = grad_out + kept["scale_two"] * (
        scaled_two - hat_two * jnp.mean(scaled_two * hat_two, axis=1, keepdims=True)
    )
    grad_mix = (kept["valid_mask"] * grad_middle).astype(BF16)
    grad_out_w = over_rows(kept["gated_mix"], grad_mix)
    grad_gated = by_rows(grad_mix, out_all)
    grad_c = grad_gated * conv_out
    grad_conv_in = grad_gated * kept["c_part"]
    grad_kernel = jnp.stack(
        [
            jnp.sum(grad_conv_in * extended[:tok_rows], axis=0),
            jnp.sum(grad_conv_in * extended[1 : tok_rows + 1], axis=0),
            jnp.sum(grad_conv_in * extended[2:], axis=0),
        ]
    )
    padded_grad = jnp.pad(grad_conv_in, ((2, 2), (0, 0)))
    grad_extended = (
        kernel[0] * padded_grad[2 : tok_rows + 4]
        + kernel[1] * padded_grad[1 : tok_rows + 3]
        + kernel[2] * padded_grad[: tok_rows + 2]
    )
    returned = shifted(grad_extended[:2], "seq", -1)
    grad_product = grad_extended[2:] + jnp.concatenate(
        [jnp.zeros((tok_rows - 2, feat_width), F32), returned], axis=0
    )
    grad_projected = jnp.concatenate(
        [grad_product * kept["v_part"], grad_c, grad_product * kept["b_part"]], axis=1
    ).astype(BF16)
    grad_in_w = over_rows(kept["normed_one"], grad_projected)
    grad_normed_one = by_rows(grad_projected, in_all)
    grad_gain_one = jnp.sum(grad_normed_one * hat_one, axis=0)
    scaled_one = grad_normed_one * norm_one_gain.astype(F32)
    grad_inputs = grad_middle + kept["scale_one"] * (
        scaled_one - hat_one * jnp.mean(scaled_one * hat_one, axis=1, keepdims=True)
    )
    return grad_inputs, grad_in_w, grad_out_w, grad_gain_one, grad_kernel, grad_gain_two


def in_blocks(
    inputs,
    lengths,
    norm_one_gain,
    w_in,
    conv_weight,
    w_out,
    norm_two_gain,
    w_gate,
    w_up,
    w_down,
    cotangent,
):
    width = inputs.shape[2]
    quarter = w_gate.shape[1] // 2
    down = w_down.T
    starts = [sum(PARTS[:i]) for i in range(len(PARTS))]
    ffn = [
        jnp.stack(
            [
                jnp.concatenate(
                    [
                        w[:, h * quarter + start : h * quarter + start + size]
                        for w in (w_gate, w_up, down)
                    ],
                    axis=1,
                )
                for h in range(2)
            ]
        )
        for start, size in zip(starts, PARTS)
    ]
    mixer, *weights = gather_all(jnp.concatenate([w_in, w_out], axis=1), ffn)
    mixer = mixer.reshape(width, 4 * width)
    in_all, out_all = mixer[:, : 3 * width], mixer[:, 3 * width :]
    kept = mixer_forward(
        inputs, lengths, norm_one_gain, conv_weight, norm_two_gain, in_all, out_all
    )
    grad_out = cotangent[0].astype(F32)
    grad_ffn = (kept["valid_mask"] * grad_out).astype(BF16)
    ffn_sum, normed_part, *ffn_grads = ffn_all(kept["normed_two"], grad_ffn, weights)
    ffn_out = ffn_sum.astype(BF16).astype(F32)
    result = (kept["middle"] + kept["valid_mask"] * ffn_out).astype(BF16)
    grad_inputs, grad_in_w, grad_out_w, gain_one, taps, gain_two = mixer_backward(
        kept, grad_out, normed_part, norm_one_gain, norm_two_gain, in_all, out_all
    )
    small = jnp.concatenate(
        [gain_one[None], taps, gain_two[None], jnp.zeros((3, width), F32)]
    )
    mixer_grad = jnp.concatenate(
        [grad_in_w.astype(BF16), grad_out_w.astype(BF16)], axis=1
    ).reshape(DEPTH, 2, 2, 2, 32, 4 * width)
    own, total = reduce_all(mixer_grad, small)
    sides = []
    for index in range(3):
        pieces = [
            grad[h, :, index * size : (index + 1) * size]
            for h in range(2)
            for grad, size in zip(ffn_grads, PARTS)
        ]
        sides.append(jnp.concatenate(pieces, axis=1).astype(F32))
    return (
        result[None],
        grad_inputs[None],
        total[0],
        own[:, : 3 * width],
        total[1:4],
        own[:, 3 * width :],
        total[4],
        sides[0],
        sides[1],
        sides[2].T,
    )


def anywhere(
    inputs,
    lengths,
    norm_one_gain,
    w_in,
    conv_weight,
    w_out,
    norm_two_gain,
    w_gate,
    w_up,
    w_down,
    cotangent,
):
    both = ("seq", "batch")
    in_all = lax.all_gather(w_in, both, axis=0, tiled=True)
    out_all = lax.all_gather(w_out, both, axis=0, tiled=True)
    gate_use, up_use = (
        lax.all_gather(
            lax.all_gather(w, "seq", axis=0, tiled=True), "batch", axis=1, tiled=True
        )
        for w in (w_gate, w_up)
    )
    down_use = lax.all_gather(
        lax.all_gather(w_down, "seq", axis=1, tiled=True), "batch", axis=0, tiled=True
    )
    kept = mixer_forward(
        inputs, lengths, norm_one_gain, conv_weight, norm_two_gain, in_all, out_all
    )
    rows_norm = kept["normed_two"]
    grad_out = cotangent[0].astype(F32)
    rows_grad = (kept["valid_mask"] * grad_out).astype(BF16)
    gate_val = rounded_dot(rows_norm, gate_use)
    up_val = rounded_dot(rows_norm, up_use)
    hidden = (jax.nn.silu(gate_val) * up_val).astype(BF16)
    ffn_out = rounded_dot(hidden, down_use)
    result = (kept["middle"] + kept["valid_mask"] * ffn_out).astype(BF16)
    grad_down = over_rows(hidden, rows_grad)
    grad_hidden = by_rows(rows_grad, down_use)
    sigmoid_gate = jax.nn.sigmoid(gate_val)
    slope_gate = sigmoid_gate * (1.0 + gate_val * (1.0 - sigmoid_gate))
    grad_gate = (grad_hidden * up_val * slope_gate).astype(BF16)
    grad_up = (grad_hidden * gate_val * sigmoid_gate).astype(BF16)
    grad_gate_w = over_rows(rows_norm, grad_gate)
    grad_up_w = over_rows(rows_norm, grad_up)
    normed_part = by_rows(grad_gate, gate_use) + by_rows(grad_up, up_use)

    def owned(grad, axis):
        half = lax.psum_scatter(
            grad.astype(BF16), "batch", scatter_dimension=axis, tiled=True
        ).astype(F32)
        return lax.psum_scatter(half, "seq", scatter_dimension=1 - axis, tiled=True)

    shards = owned(grad_gate_w, 1), owned(grad_up_w, 1), owned(grad_down, 0)
    grad_inputs, grad_in_w, grad_out_w, gain_one, taps, gain_two = mixer_backward(
        kept, grad_out, normed_part, norm_one_gain, norm_two_gain, in_all, out_all
    )
    shard_in, shard_out = (
        lax.psum_scatter(grad, both, scatter_dimension=0, tiled=True)
        for grad in (grad_in_w, grad_out_w)
    )
    total_one, total_two, total_kernel = lax.psum((gain_one, gain_two, taps), both)
    return (
        result[None],
        grad_inputs[None],
        total_one,
        shard_in,
        total_kernel,
        shard_out,
        total_two,
    ) + shards


def solution(mesh):
    in_specs = (
        P("batch", "seq", None),
        P("batch"),
        P(),
        P(("seq", "batch"), None),
        P(),
        P(("seq", "batch"), None),
        P(),
        P("seq", "batch"),
        P("seq", "batch"),
        P("batch", "seq"),
        P("batch", "seq", None),
    )
    out_specs = (
        P("batch", "seq", None),
        P("batch", "seq", None),
        P(),
        P(("seq", "batch"), None),
        P(),
        P(("seq", "batch"), None),
        P(),
        P("seq", "batch"),
        P("seq", "batch"),
        P("batch", "seq"),
    )
    by_blocks = mesh.shape["seq"] == 4 * DEPTH and mesh.shape["batch"] == 2
    return jax.shard_map(
        in_blocks if by_blocks else anywhere,
        mesh=mesh,
        in_specs=in_specs,
        out_specs=out_specs,
        check_vma=False,
    )
```

time: 1660 us -> 483 us (0.29)
  waiting for transfers between devices: 1430 us -> 0.01 us
  Pallas kernels: 0 us -> 392 us
  matrix products: 121 us -> 28 us
  blocking collectives: 40.6 us -> 0 us
    reduce_scatter x7 -> x0, waiting for transfers between devices: 709 us -> none  [the longest x1 159 us: on_device(): lax.psum_scatter(grad_in_w, ('seq', 'batch'), scatter_dimension=0, tiled=...]
    all_gather x8 -> x0, waiting for transfers between devices: 602 us -> none  [the longest x1 112 us: on_device(): lax.all_gather(up_seq, 'batch', axis=1, tiled=True)]
    pallas_call x0 -> x3, Pallas kernels: none -> 392 us  [the longest x1 179 us: ffn_all(): pl.pallas_call(ffn_kernel, out_shape=out_shape, in_specs=[vmem, vmem, hbm...]
    unnamed x17 -> x0, waiting for transfers between devices: 119 us -> none
    psum x1 -> x0, blocking collectives: 40.6 us -> none  [on_device(): lax.psum((grad_gain_one, grad_gain_two, grad_kernel), ('seq', 'batch'))]
    dot_general x5 -> x2, matrix products: 44.6 us -> 8 us  [by_rows(): lax.dot_general(left, right, (((1,), (1,)), ((), ())), preferred_element_...]
    dot_general x5 -> x2, matrix products: 36.7 us -> 8.6 us  [over_rows(): lax.dot_general(left, right, (((0,), (0,)), ((), ())), preferred_element_...]
    dot_general x5 -> x2, matrix products: 39.5 us -> 11.5 us  [dot(): return jnp.dot(left, right, preferred_element_type=F32)]
  transfers between devices with their start and end apart: 18 -> 2, of which waited for: 18 -> 0; matrix products, arithmetic and copies ran while one was open for 9% -> 1% of each run, Pallas kernels for 0% -> 0%
where the time goes in v1:
time: 483 us; the launch traced here: 477 us
  Pallas kernels  392 us (81%)
  other arithmetic  28.8 us (6%)
  matrix products  28 us (6%)
  local copies, waits for them, and re-layouts  23.5 us (5%)
    pallas_call x1, Pallas kernels, ffn_all(): pl.pallas_call(ffn_kernel, out_shape=out_shape, in_specs=[vmem, vmem, hbm...  179 us
    pallas_call x1, Pallas kernels, gather_all(): pl.pallas_call(gather_kernel, out_shape=shapes, in_specs=[vmem] * 4, out_...  153 us
    pallas_call x1, Pallas kernels, reduce_all(): pl.pallas_call(reduce_kernel, out_shape=[jax.ShapeDtypeStruct((32, column...  60.5 us
    unnamed x59, local copies, waits for them, and re-layouts  12.4 us
    dot_general x2, matrix products, dot(): return jnp.dot(left, right, preferred_element_type=F32)  11.5 us
  transfers between devices with their start and end apart: 2, of which 0 were waited for; matrix products, arithmetic and copies ran while one was open for 1% of the time, Pallas kernels for 0%

profile of v1, /device:TPU:0, one launch (start us, length us, event | category | flops | bytes accessed | tf_op | source)
XLA Modules:
  0.0 477.0 jit_solution(1475817462186345441)
XLA Ops:
  0.7 0.9 fusion.43
  9.2 152.5 %shard_map.186 = (bf16[4,2,2,2,32,4096]{5,4,3,2,1,0:T(8,128)(2,1)}, bf16[4,2,2,64,1536]{4,3,2,1,0:T(8,128)(2,1)S(1)}, bf16[4,2,2,64,1152]{4,3,2,1,0:T(8,128)(2,1)S(1)}, bf16[4,2,2,64,768]{4,3,2,1,0:T(8,128)(2,1)S(1)}) custom-call(bf16[32,4096]{1,0:T(8,128)(2,1)S(1)} %pad_maximum_fusion.6.mixer_ref, bf16[2,64,1536]{2,1,0:T(8,128)(2,1)S(1)} %pad_maximum_fusion.4.f0_ref, ...), custom_call_target="tpu_custom_call" | custom-call | tf_op jit(solution)/shard_map/pallas_call | solution.py:371
  161.8 8.1 %fusion.7 = f32[512,3072]{1,0:T(8,128)S(1)} fusion(bf16[1024,4096]{1,0:T(8,128)(2,1)} %bitcast.104, bf16[1,512,1024]{2,1,0:T(8,128)(2,1)S(1)} %copy-done.13, f32[1024]{0:T(1024)S(1)} %convert_element_type.91, f32[512]{0:T(512)S(1)} %add_rsqrt_fusion.1), kind=kOutput, calls=%fused_computation.7 | convolution fusion | flops 3226468352 | bytes 13637632 | tf_op jit(solution)/shard_map/dot_general | solution.py:30
  170.3 2.3 copy-done.6
  172.6 1.4 collective-permute-start
  174.7 1.2 fusion.14.grad_ref
  176.3 4.4 multiply_convert_fusion.5
  180.7 3.4 multiply_reduce_fusion.5
  184.1 1.3 copy-done.7
  185.4 1.2 multiply_convert_fusion.4.normed_ref
  186.7 178.7 %shard_map.187 = (f32[512,1024]{1,0:T(8,128)}, f32[512,1024]{1,0:T(8,128)}, bf16[2,64,1536]{2,1,0:T(8,128)(2,1)}, bf16[2,64,1152]{2,1,0:T(8,128)(2,1)}, bf16[2,64,768]{2,1,0:T(8,128)(2,1)}) custom-call(bf16[512,1024]{1,0:T(8,128)(2,1)} %multiply_convert_fusion.4.normed_ref, bf16[512,1024]{1,0:T(8,128)(2,1)} %fusion.14.grad_ref, ...), custom_call_target="tpu_custom_call" | custom-call | tf_op jit(solution)/shard_map/pallas_call | solution.py:598
  365.3 1.1 bitcast_dynamic-update-slice_fusion.1
  371.6 2.5 multiply_reduce_fusion
  374.1 3.5 convert_add_fusion.1
  377.6 3.0 fusion.23
  380.7 1.3 multiply_reduce_fusion.1
  382.7 1.6 collective-permute-start.1
  384.3 2.6 convolution_convert_fusion.1
  389.9 5.0 %fusion.21 = (f32[1024]{0:T(1024)S(1)}, f32[512]{0:T(512)S(1)}, f32[512,1024]{1,0:T(8,128)}) fusion(bf16[1,512,1024]{2,1,0:T(8,128)(2,1)S(1)} %copy-done.14, f32[512]{0:T(512)S(1)} %add_rsqrt_fusion.1, f32[1024]{0:T(1024)S(1)} %convert_element_type.91, bf16[1024,4096]{1,0:T(8,128)(2,1)S(1)} %bitcast.109, bf16[512,1024]{1,0:T(8,128)(2,1)S(1)} %get-tuple-element.43, ...), kind=kOutput, calls=%fused_computation.26 | convolution fusion | flops 3234331136 | bytes 12595200 | tf_op jit(solution)/shard_map/dot_general | solution.py:24
  394.8 6.0 %convolution_convert_fusion = bf16[1024,3072]{1,0:T(8,128)(2,1)} fusion(bf16[512,1024]{1,0:T(8,128)(2,1)S(1)} %get-tuple-element.43, bf16[512,1024]{1,0:T(8,128)(2,1)S(1)} %get-tuple-element.44, bf16[512,1024]{1,0:T(8,128)(2,1)S(1)} %get-tuple-element.42, bf16[1,512,1024]{2,1,0:T(8,128)(2,1)S(1)} %copy-done.14, f32[1024]{0:T(1024)S(1)} %convert_element_type.91, ...), kind=kOutput, calls=%fused_computation.1 | convolution fusion | flops 3235905536 | bytes 10491904 | tf_op jit(solution)/shard_map/dot_general | solution.py:18
  400.8 7.6 %pad_maximum_fusion = bf16[1024,4096]{1,0:T(8,128)(2,1)} fusion(bf16[1024,1024]{1,0:T(8,128)(2,1)} %convolution_convert_fusion.1, bf16[1024,3072]{1,0:T(8,128)(2,1)} %convolution_convert_fusion), kind=kLoop, calls=%fused_computation | loop fusion | flops 16777216 | bytes 16777216 | tf_op jit(solution)/shard_map/concatenate | solution.py:827
  408.5 3.4 copy-done
  411.8 60.5 %shard_map.188 = (f32[32,4096]{1,0:T(8,128)S(1)}, f32[8,1024]{1,0:T(8,128)S(1)}) custom-call(bf16[4,2,2,2,32,4096]{5,4,3,2,1,0:T(8,128)(2,1)S(1)} %bitcast.85, f32[8,1024]{1,0:T(8,128)S(1)} %concatenate.57.small_ref), custom_call_target="tpu_custom_call" | custom-call | tf_op jit(solution)/shard_map/pallas_call | solution.py:670
  475.0 1.9 fusion.20
  (99 shorter events, 19.7 us)
Async XLA Ops:
  0.6 7.6 %copy-start.13 = (bf16[1,512,1024]{2,1,0:T(8,128)(2,1)S(1)}, bf16[1,512,1024]{2,1,0:T(8,128)(2,1)}, u32[]{:S(2)}) copy-start(bf16[1,512,1024]{2,1,0:T(8,128)(2,1)} %param.11) | copy-start | bytes 3145732
  0.7 7.9 %copy-start.21 = (bf16[1024]{0:T(1024)(128)(2,1)S(1)}, bf16[1024]{0:T(1024)(128)(2,1)}, u32[]{:S(2)}) copy-start(bf16[1024]{0:T(1024)(128)(2,1)} %param.13) | copy-start | bytes 6148
  161.8 8.1 %copy-start.1 = (bf16[4,2,2,64,1536]{4,3,2,1,0:T(8,128)(2,1)}, bf16[4,2,2,64,1536]{4,3,2,1,0:T(8,128)(2,1)S(1)}, u32[]{:S(2)}) copy-start(bf16[4,2,2,64,1536]{4,3,2,1,0:T(8,128)(2,1)S(1)} %get-tuple-element.22.w0_ref) | copy-start | bytes 9437188
  161.8 8.1 %copy-start.2 = (bf16[4,2,2,64,1152]{4,3,2,1,0:T(8,128)(2,1)}, bf16[4,2,2,64,1152]{4,3,2,1,0:T(8,128)(2,1)S(1)}, u32[]{:S(2)}) copy-start(bf16[4,2,2,64,1152]{4,3,2,1,0:T(8,128)(2,1)S(1)} %get-tuple-element.23.w1_ref) | copy-start | bytes 7077892
  161.8 8.1 %copy-start.3 = (bf16[4,2,2,64,768]{4,3,2,1,0:T(8,128)(2,1)}, bf16[4,2,2,64,768]{4,3,2,1,0:T(8,128)(2,1)S(1)}, u32[]{:S(2)}) copy-start(bf16[4,2,2,64,768]{4,3,2,1,0:T(8,128)(2,1)S(1)} %get-tuple-element.24.w2_ref) | copy-start | bytes 4718596
  169.9 2.7 copy-start.6
  169.9 4.8 %copy-start.11 = (bf16[1,512,1024]{2,1,0:T(8,128)(2,1)S(1)}, bf16[1,512,1024]{2,1,0:T(8,128)(2,1)}, u32[]{:S(2)}) copy-start(bf16[1,512,1024]{2,1,0:T(8,128)(2,1)} %param.21) | copy-start | bytes 3145732
  172.6 3.3 copy-start.20
  172.6 3.4 copy-start.22
  172.6 3.4 collective-permute-start
  176.3 4.4 copy-start.4
  180.7 3.4 copy-start.16
  365.3 6.2 %copy-start.8 = (f32[512,1024]{1,0:T(8,128)S(1)}, f32[512,1024]{1,0:T(8,128)}, u32[]{:S(2)}) copy-start(f32[512,1024]{1,0:T(8,128)} %copy-done.7) | copy-start | bytes 6291460
  370.7 3.4 copy-start.9
  370.7 3.4 copy-start.12
  371.6 9.1 %slice-start = ((s8[6291456]{0:T(1024)(128)(4,1)}), s8[4194304]{0:T(1024)(128)(4,1)S(1)}, s32[]{:S(2)}) async-start(s8[6291456]{0:T(1024)(128)(4,1)} %bitcast.86), calls=%async_computation | async-start | bytes 8388608
  374.1 6.6 %slice-start.1 = ((s8[6291456]{0:T(1024)(128)(4,1)}), s8[2097152]{0:T(1024)(128)(4,1)S(1)}, s32[]{:S(2)}) async-start(s8[6291456]{0:T(1024)(128)(4,1)} %bitcast.86), calls=%async_computation.1 | async-start | bytes 4194304
  377.6 3.1 copy-start.5
  377.6 3.1 copy-start.10
  382.1 7.4 %slice-start.2 = ((s8[8388608]{0:T(1024)(128)(4,1)}), s8[4194304]{0:T(1024)(128)(4,1)S(1)}, s32[]{:S(2)}) async-start(s8[8388608]{0:T(1024)(128)(4,1)} %bitcast.107), calls=%async_computation.2 | async-start | bytes 8388608
  382.7 6.8 %slice-start.3 = ((s8[8388608]{0:T(1024)(128)(4,1)}), s8[4194304]{0:T(1024)(128)(4,1)S(1)}, s32[]{:S(2)}) async-start(s8[8388608]{0:T(1024)(128)(4,1)} %bitcast.107), calls=%async_computation.3 | async-start | bytes 8388608
  382.7 5.9 %collective-permute-start.1 = (f32[2,1024]{1,0:T(2,128)S(1)}, f32[2,1024]{1,0:T(2,128)S(1)}, u32[]{:S(2)}, u32[]{:S(2)}) collective-permute-start(f32[2,1024]{1,0:T(2,128)S(1)} %slice.257), channel_id=1, source_target_pairs={{2,0},{4,2},{6,4},{8,6},{10,8},{12,10},{14,12},{16,14},{18,16},{20... | collective-permute-start | bytes 24584 | tf_op jit(solution)/shard_map/ppermute | solution.py:698
  408.5 3.4 copy-start
  411.8 63.1 %copy-start.15 = (f32[512,1024]{1,0:T(8,128)S(1)}, f32[512,1024]{1,0:T(8,128)}, u32[]{:S(2)}) copy-start(f32[512,1024]{1,0:T(8,128)} %get-tuple-element.90) | copy-start | bytes 6291460
  (5 other events, 6.7 us)
